TPU v7x, 32 devices: a whole 2x2x4 slice. The times are simulated.
32 devices in a mesh: row: 4 (over y, core), col: 8 (over z, x).
Axes of the slice: x: 2, y: 2, z: 4, core: 2. Of those that a mesh axis runs over, the one named last changes fastest.
Arguments:
- snapshots: bfloat16 [64, 384, 1024], P(None, 'row', 'col'), may hold values from -870 to 870
Outputs:
- q_blocks: float32 [64, 384, 1024], P(None, 'row', 'col')
- r_factor: float32 [64, 64], replicated
All inputs are finite; a program needn't handle non-finite values.
Results may differ from a plain program's by a relative error of at most 0.0003.
Values may be sent and summed in bfloat16 or wider, within the bound.
A program may use at most 64 MiB of HBM per device.

v0:
```python
import jax
import jax.numpy as jnp
from jax import lax
from jax.sharding import PartitionSpec as P

HALF = 16


def padded(array, sides, width):
    for axis, dim in sides:
        devices, length = (lax.axis_size(axis), array.shape[dim])
        up = [(i, (i + 1) % devices) for i in range(devices)]
        down = [(j, i) for i, j in up]
        last = lax.slice_in_dim(array, length - width, length, axis=dim)
        initial = lax.slice_in_dim(array, 0, width, axis=dim)
        before = lax.ppermute(last, axis, up)
        after = lax.ppermute(initial, axis, down)
        array = jnp.concatenate([before, array, after], axis=dim)
    return array


def band_matrix(length):
    sigma = HALF / 3.0
    offsets = jnp.arange(2 * HALF + 1, dtype=jnp.float32) - HALF
    total = jnp.sum(jnp.exp(-offsets * offsets / (2.0 * sigma * sigma)))
    outer = jnp.arange(length + 2 * HALF)[:, None]
    inner = jnp.arange(length)[None, :]
    spread = outer - inner
    shifted = (spread - HALF).astype(jnp.float32)
    inside = (spread >= 0) & (spread <= 2 * HALF)
    return jnp.where(inside, jnp.exp(-shifted * shifted / (2.0 * sigma * sigma)) / total, 0.0)


def filter_columns(field):
    width = field.shape[2] - 2 * HALF
    return jnp.einsum("src,cd->srd", field, band_matrix(width), precision=lax.Precision.HIGHEST)


def filter_rows(field):
    height = field.shape[1] - 2 * HALF
    return jnp.einsum("src,rq->sqc", field, band_matrix(height), precision=lax.Precision.HIGHEST)


def local(snapshots):
    count, height, width = snapshots.shape
    extended = padded(snapshots, (("row", 1), ("col", 2)), HALF)
    filtered = filter_rows(filter_columns(extended.astype(jnp.float32)))
    points = height * width * lax.axis_size("row") * lax.axis_size("col")
    flat_field = filtered.reshape(count, height * width)
    local_gram = jnp.dot(flat_field, flat_field.T, precision=lax.Precision.HIGHEST) / points
    gram = lax.psum(local_gram, ("row", "col"))
    upper = jnp.linalg.cholesky(gram).T
    basis = lax.linalg.triangular_solve(upper.T, flat_field, left_side=True, lower=True)
    return (basis.reshape(count, height, width), upper)


def solution(mesh):
    return jax.shard_map(
        local,
        mesh=mesh,
        in_specs=(P(None, "row", "col"),),
        out_specs=(P(None, "row", "col"), P()),
        check_vma=False,
    )
```

profile of v0, /device:TPU:0, one launch (start us, length us, event | category | flops | bytes accessed | tf_op | source)
XLA Modules:
  0.0 109.6 jit_solution(14861806101442300612)
XLA Ops:
  0.6 1.1 fusion.77
  1.7 2.5 %collective-permute-start.1 = (bf16[64,16,128]{2,1,0:T(8,128)(2,1)S(1)}, bf16[64,16,128]{2,1,0:T(8,128)(2,1)S(1)}, u32[]{:S(2)}, u32[]{:S(2)}) collective-permute-start(bf16[64,16,128]{2,1,0:T(8,128)(2,1)S(1)} %get-tuple-element.13), channel_id=1, source_target_pairs={{8,0},{16,8},{24,16},{0,24},{9,1},{17,9},{25,17},{1,25},{10,2},{18... | collective-permute-start | bytes 786440 | tf_op jit(solution)/shard_map/ppermute | solution.py:17
  4.2 0.0 collective-permute-start
  4.2 3.1 %copy.30 = bf16[64,96,128]{1,2,0:T(8,128)(2,1)S(1)} copy(bf16[64,96,128]{2,1,0:T(8,128)(2,1)} %param.1) | data formatting | bytes 3145728 | tf_op args[0]
  7.3 3.5 %collective-permute-done.1 = bf16[64,16,128]{2,1,0:T(8,128)(2,1)S(1)} collective-permute-done((bf16[64,16,128]{2,1,0:T(8,128)(2,1)S(1)}, bf16[64,16,128]{2,1,0:T(8,128)(2,1)S(1)}, u32[]{:S(2)}, u32[]{:S(2)}) %collective-permute-start.1) | collective-permute-done | bytes 262176 | tf_op jit(solution)/shard_map/ppermute | solution.py:17
  10.8 1.7 %copy.31 = bf16[64,16,128]{1,2,0:T(8,128)(2,1)} copy(bf16[64,16,128]{2,1,0:T(8,128)(2,1)S(1)} %collective-permute-done.1) | data formatting | bytes 524288 | tf_op jit(solution)/shard_map/ppermute | solution.py:17
  12.5 0.0 collective-permute-done
  12.5 1.8 %copy.29 = bf16[64,16,128]{1,2,0:T(8,128)(2,1)} copy(bf16[64,16,128]{2,1,0:T(8,128)(2,1)S(1)} %collective-permute-done) | data formatting | bytes 524288 | tf_op jit(solution)/shard_map/ppermute | solution.py:16
  14.3 0.0 copy-start
  14.3 0.0 copy-start.1
  14.3 1.8 %pad_maximum_fusion.2 = (bf16[64,128,16]{1,2,0:T(8,128)(2,1)S(1)}, bf16[64,128,16]{1,2,0:T(8,128)(2,1)S(1)}) fusion(bf16[64,16,128]{1,2,0:T(8,128)(2,1)} %copy.31, bf16[64,96,128]{1,2,0:T(8,128)(2,1)S(1)} %copy.30, bf16[64,16,128]{1,2,0:T(8,128)(2,1)} %copy.29), kind=kLoop, calls=%fused_computation.20 | loop fusion | flops 1572864 | bytes 2621440 | tf_op jit(solution)/shard_map/slice | solution.py:14
  16.1 1.5 %collective-permute-start.2 = (bf16[64,128,16]{1,2,0:T(8,128)(2,1)S(1)}, bf16[64,128,16]{1,2,0:T(8,128)(2,1)S(1)}, u32[]{:S(2)}, u32[]{:S(2)}) collective-permute-start(bf16[64,128,16]{1,2,0:T(8,128)(2,1)S(1)} %get-tuple-element.10), channel_id=1, source_target_pairs={{0,1},{1,2},{2,3},{3,4},{4,5},{5,6},{6,7},{7,0},{8,9},{9,10},{10,1... | collective-permute-start | bytes 786440 | tf_op jit(solution)/shard_map/ppermute | solution.py:16
  17.7 3.2 %collective-permute-start.3 = (bf16[64,128,16]{1,2,0:T(8,128)(2,1)S(1)}, bf16[64,128,16]{1,2,0:T(8,128)(2,1)S(1)}, u32[]{:S(2)}, u32[]{:S(2)}) collective-permute-start(bf16[64,128,16]{1,2,0:T(8,128)(2,1)S(1)} %get-tuple-element.11), channel_id=1, source_target_pairs={{1,0},{2,1},{3,2},{4,3},{5,4},{6,5},{7,6},{0,7},{9,8},{10,9},{11,1... | collective-permute-start | bytes 786440 | tf_op jit(solution)/shard_map/ppermute | solution.py:17
  20.9 0.6 fusion.65
  21.5 7.8 %collective-permute-done.2 = bf16[64,128,16]{1,2,0:T(8,128)(2,1)S(1)} collective-permute-done((bf16[64,128,16]{1,2,0:T(8,128)(2,1)S(1)}, bf16[64,128,16]{1,2,0:T(8,128)(2,1)S(1)}, u32[]{:S(2)}, u32[]{:S(2)}) %collective-permute-start.2) | collective-permute-done | bytes 262176 | tf_op jit(solution)/shard_map/ppermute | solution.py:16
  29.4 2.2 %collective-permute-done.3 = bf16[64,128,16]{1,2,0:T(8,128)(2,1)S(1)} collective-permute-done((bf16[64,128,16]{1,2,0:T(8,128)(2,1)S(1)}, bf16[64,128,16]{1,2,0:T(8,128)(2,1)S(1)}, u32[]{:S(2)}, u32[]{:S(2)}) %collective-permute-start.3) | collective-permute-done | bytes 262176 | tf_op jit(solution)/shard_map/ppermute | solution.py:17
  31.6 0.0 copy-done
  31.6 0.0 copy-done.1
  31.6 7.8 %fusion.5 = f32[64,128,128]{2,1,0:T(8,128)S(1)} fusion(bf16[64,128,16]{1,2,0:T(8,128)(2,1)S(1)} %collective-permute-done.3, bf16[64,16,128]{1,2,0:T(8,128)(2,1)S(1)} %copy-done, bf16[64,96,128]{1,2,0:T(8,128)(2,1)S(1)} %copy.30, bf16[64,16,128]{1,2,0:T(8,128)(2,1)S(1)} %copy-done.1, bf16[64,128,16]{1,2,0:T(8,128)(2,1)S(1)} %collective-permute-done.2, f32[]{:T(128)} %fusion.65), kind=kOutput, calls=%fused_computation.6 | convolution fusion | flops 2026598400 | bytes 6815748 | tf_op jit(solution)/shard_map/src,cd->srd/dot_general | solution.py:36
  39.3 3.7 %fusion.39 = f32[96,64,128]{2,0,1:T(8,128)S(1)} fusion(f32[64,128,128]{2,1,0:T(8,128)S(1)} %fusion.5, f32[]{:T(128)} %fusion.65), kind=kOutput, calls=%fused_computation.39 | convolution fusion | flops 1208094720 | bytes 7340036 | tf_op jit(solution)/shard_map/src,rq->sqc/dot_general | solution.py:41
  43.1 6.1 %fusion.18 = f32[64,64]{0,1:T(8,128)S(1)} fusion(f32[64,96,128]{2,1,0:T(8,128)S(1)} %bitcast.38), kind=kOutput, calls=%fused_computation.17 | convolution fusion | flops 603983872 | bytes 3162112 | tf_op jit(solution)/shard_map/dot_general | solution.py:50
  49.2 39.4 %psum.7 = f32[64,64]{0,1:T(8,128)S(1)} all-reduce(f32[64,64]{0,1:T(8,128)S(1)} %fusion.18), channel_id=1, replica_groups=mesh['row'=4,'col'=8] {'row','col'}, use_global_device_ids=true, to_apply=%region_1.2 | all-reduce | flops 4096 | bytes 32768 | tf_op jit(solution)/shard_map/psum | solution.py:51
  88.6 0.1 copy.35
  88.7 5.8 %cholesky.16 = f32[64,64]{1,0:T(8,128)S(1)} custom-call(f32[64,64]{1,0:T(8,128)S(1)} %fusion.55), custom_call_target="Cholesky" | custom-call | tf_op jit(solution)/shard_map/jit(cholesky)/cholesky | solution.py:52
  94.6 0.6 compare_reduce_fusion
  95.3 0.7 fusion.56
  95.9 0.7 copy.39
  96.6 4.9 %custom-call.6 = f32[1,64,64]{1,2,0:T(8,128)S(1)} custom-call(f32[1,64,64]{2,1,0:T(8,128)S(1)} %get-tuple-element.15), custom_call_target="InvertDiagBlocksLowerTriangular" | custom-call | tf_op jit(solution)/shard_map/triangular_solve | solution.py:53
  101.5 4.6 %fusion = f32[64,96,128]{2,0,1:T(8,128)S(1)} fusion(f32[1,64,64]{1,2,0:T(8,128)S(1)} %custom-call.6, f32[8,8,96,128]{3,2,1,0:T(8,128)S(1)} %bitcast.39), kind=kOutput, calls=%fused_computation.1 | convolution fusion | flops 603979776 | bytes 6307840 | tf_op jit(solution)/shard_map/triangular_solve | solution.py:53
  106.1 3.5 %copy.38 = f32[64,96,128]{2,1,0:T(8,128)} copy(f32[64,96,128]{2,0,1:T(8,128)S(1)} %fusion) | data formatting | bytes 6291456
  (2 shorter events, 0.0 us)
Async XLA Ops:
  1.7 9.1 %collective-permute-start.1 = (bf16[64,16,128]{2,1,0:T(8,128)(2,1)S(1)}, bf16[64,16,128]{2,1,0:T(8,128)(2,1)S(1)}, u32[]{:S(2)}, u32[]{:S(2)}) collective-permute-start(bf16[64,16,128]{2,1,0:T(8,128)(2,1)S(1)} %get-tuple-element.13), channel_id=1, source_target_pairs={{8,0},{16,8},{24,16},{0,24},{9,1},{17,9},{25,17},{1,25},{10,2},{18... | collective-permute-start | bytes 786440 | tf_op jit(solution)/shard_map/ppermute | solution.py:17
  4.2 8.4 %collective-permute-start = (bf16[64,16,128]{2,1,0:T(8,128)(2,1)S(1)}, bf16[64,16,128]{2,1,0:T(8,128)(2,1)S(1)}, u32[]{:S(2)}, u32[]{:S(2)}) collective-permute-start(bf16[64,16,128]{2,1,0:T(8,128)(2,1)S(1)} %get-tuple-element.12), channel_id=1, source_target_pairs={{0,8},{8,16},{16,24},{24,0},{1,9},{9,17},{17,25},{25,1},{2,10},{10... | collective-permute-start | bytes 786440 | tf_op jit(solution)/shard_map/ppermute | solution.py:16
  14.3 17.3 %copy-start = (bf16[64,16,128]{1,2,0:T(8,128)(2,1)S(1)}, bf16[64,16,128]{1,2,0:T(8,128)(2,1)}, u32[]{:S(2)}) copy-start(bf16[64,16,128]{1,2,0:T(8,128)(2,1)} %copy.31) | copy-start | bytes 786436
  14.3 17.3 %copy-start.1 = (bf16[64,16,128]{1,2,0:T(8,128)(2,1)S(1)}, bf16[64,16,128]{1,2,0:T(8,128)(2,1)}, u32[]{:S(2)}) copy-start(bf16[64,16,128]{1,2,0:T(8,128)(2,1)} %copy.29) | copy-start | bytes 786436
  16.1 13.2 %collective-permute-start.2 = (bf16[64,128,16]{1,2,0:T(8,128)(2,1)S(1)}, bf16[64,128,16]{1,2,0:T(8,128)(2,1)S(1)}, u32[]{:S(2)}, u32[]{:S(2)}) collective-permute-start(bf16[64,128,16]{1,2,0:T(8,128)(2,1)S(1)} %get-tuple-element.10), channel_id=1, source_target_pairs={{0,1},{1,2},{2,3},{3,4},{4,5},{5,6},{6,7},{7,0},{8,9},{9,10},{10,1... | collective-permute-start | bytes 786440 | tf_op jit(solution)/shard_map/ppermute | solution.py:16
  17.7 13.9 %collective-permute-start.3 = (bf16[64,128,16]{1,2,0:T(8,128)(2,1)S(1)}, bf16[64,128,16]{1,2,0:T(8,128)(2,1)S(1)}, u32[]{:S(2)}, u32[]{:S(2)}) collective-permute-start(bf16[64,128,16]{1,2,0:T(8,128)(2,1)S(1)} %get-tuple-element.11), channel_id=1, source_target_pairs={{1,0},{2,1},{3,2},{4,3},{5,4},{6,5},{7,6},{0,7},{9,8},{10,9},{11,1... | collective-permute-start | bytes 786440 | tf_op jit(solution)/shard_map/ppermute | solution.py:17
where the time goes:
time: 110 us
  blocking collectives  39.4 us (36%)
  matrix products  22.2 us (20%)
  other arithmetic  14.5 us (13%)
  waiting for transfers between devices  13.6 us (12%)
  local copies, waits for them, and re-layouts  11.9 us (11%)
  starting transfers between devices  7.24 us (7%)
    psum x1, blocking collectives, local(): gram = lax.psum(local_gram, ('row', 'col'))  39.4 us
    ppermute x2, waiting for transfers between devices, padded(): before = lax.ppermute(last, axis, up)  7.82 us
    dot_general x1, matrix products, filter_columns(): jnp.einsum('src,cd->srd', field, band_matrix(width), precision=lax.Precis...  7.76 us
    unnamed x7, local copies, waits for them, and re-layouts  7.3 us
    another operation x3, other arithmetic, local(): upper = jnp.linalg.cholesky(gram).T  6.52 us
    dot_general x1, matrix products, local(): jnp.dot(flat_field, flat_field.T, precision=lax.Precision.HIGHEST) / points  6.13 us
    ppermute x2, waiting for transfers between devices, padded(): after = lax.ppermute(initial, axis, down)  5.73 us
    ppermute x2, starting transfers between devices, padded(): after = lax.ppermute(initial, axis, down)  5.69 us
  transfers between devices with their start and end apart: 4, of which 3 were waited for; matrix products, arithmetic and copies ran while one was open for 5% of the time, Pallas kernels for 0%

commit v1 on v0

v1 whole, which is shorter than its diff:
```python
import functools

import jax
import jax.numpy as jnp
import ml_dtypes
import numpy as np
from jax import lax
from jax.experimental import pallas as pl
from jax.experimental.pallas import tpu as pltpu
from jax.sharding import PartitionSpec as P

HALF = 16
F32, BF16 = jnp.float32, jnp.bfloat16
MESH = pl.DeviceIdType.MESH


def taps():
    sigma = HALF / 3.0
    offsets = np.arange(2 * HALF + 1, dtype=np.float64) - HALF
    weights = np.exp(-offsets * offsets / (2.0 * sigma * sigma))
    return (weights / weights.sum()).astype(np.float32)


def split_terms(values):
    high = values.astype(ml_dtypes.bfloat16)
    low = (values - high.astype(np.float32)).astype(ml_dtypes.bfloat16)
    return high, low


def band(length):
    weights = taps()
    result = np.zeros((length + 2 * HALF, length), np.float32)
    for j in range(length):
        result[j : j + 2 * HALF + 1, j] = weights
    return result


def constants(height, width):
    fold = width // HALF
    across = band(width)
    own = across[HALF : HALF + width]
    left, right = across[:HALF], across[HALF + width :]
    own_w = np.concatenate(split_terms(own), axis=0)
    strip = np.zeros((2, fold, HALF, fold, width), np.float32)
    for s in range(fold):
        strip[0, s, :, s] = left
        strip[1, s, :, s] = right
    strip_w = np.concatenate(split_terms(strip.reshape(2 * width, fold * width)), axis=0)
    pick = np.zeros((fold, width, 2, fold, HALF), np.float32)
    for s in range(fold):
        for c in range(HALF):
            pick[s, c, 0, s, c] = 1.0
            pick[s, width - HALF + c, 1, s, c] = 1.0
    pick = pick.reshape(fold * width, 2 * width).astype(ml_dtypes.bfloat16)
    high, low = split_terms(np.ascontiguousarray(band(height).T))
    rows_w = np.concatenate([high, high, low], axis=1)
    return pick, own_w, strip_w, rows_w


def split_value(value):
    high = value.astype(BF16)
    return high, (value - high.astype(F32)).astype(BF16)


def dot(a, b):
    return jnp.dot(a, b, preferred_element_type=F32)


def filter_kernel(rows, cols, x_ref, pick_hbm, own_hbm, strip_hbm, band_hbm, field_hbm, gram_ref,
                  ext, sides, packed, pick, own_w, strip_w, band_w, filtered, field, slots_r, slots_c,
                  load_sem, send_sem, recv_sem, send_r, recv_r, send_c, recv_c, out_sem):
    count, height, width = x_ref.shape
    tall = height + 2 * HALF
    fold = width // HALF
    groups = count // fold
    me_r, me_c = lax.axis_index("row"), lax.axis_index("col")
    up, down = lax.rem(me_r + rows - 1, rows), lax.rem(me_r + 1, rows)
    left, right = lax.rem(me_c + cols - 1, cols), lax.rem(me_c + 1, cols)

    body = pl.ds(HALF, height)
    loads = [
        pltpu.make_async_copy(x_ref, ext.at[:, body, :], load_sem.at[0]),
        pltpu.make_async_copy(pick_hbm, pick, load_sem.at[1]),
        pltpu.make_async_copy(own_hbm, own_w, load_sem.at[2]),
        pltpu.make_async_copy(strip_hbm, strip_w, load_sem.at[3]),
        pltpu.make_async_copy(band_hbm, band_w, load_sem.at[4]),
    ]
    for load in loads:
        load.start()

    barrier = pltpu.get_barrier_semaphore()
    friends = [(lax.rem(me_r + k, rows), me_c) for k in range(1, rows)]
    friends += [(me_r, lax.rem(me_c + k, cols)) for k in range(1, cols)]
    friends += [(up, left), (up, right), (down, left), (down, right)]
    for friend in friends:
        pl.semaphore_signal(barrier, inc=1, device_id=friend, device_id_type=MESH)

    loads[0].wait()
    loads[1].wait()

    def pack(g, carry):
        planes = [ext[g * fold + s, HALF : HALF + height, :] for s in range(fold)]
        strips = dot(jnp.concatenate(planes, axis=1), pick[...]).astype(BF16)
        packed[0, g] = strips[:, :width]
        packed[1, g] = strips[:, width:]
        return carry

    lax.fori_loop(0, groups, pack, 0)
    pl.semaphore_wait(barrier, len(friends))

    top, bottom = pl.ds(0, HALF), pl.ds(height - HALF, HALF)
    far = pl.ds(HALF + height, HALF)

    def remote(index, src, dst, device):
        return pltpu.make_async_remote_copy(
            src_ref=src, dst_ref=dst, send_sem=send_sem.at[index], recv_sem=recv_sem.at[index],
            device_id=device, device_id_type=MESH)

    copies = [
        remote(0, packed.at[0], sides.at[1, :, body, :], (me_r, left)),
        remote(1, packed.at[1], sides.at[0, :, body, :], (me_r, right)),
        remote(2, x_ref.at[:, top, :], ext.at[:, far, :], (up, me_c)),
        remote(3, x_ref.at[:, bottom, :], ext.at[:, pl.ds(0, HALF), :], (down, me_c)),
        remote(4, packed.at[0, :, top, :], sides.at[1, :, far, :], (up, left)),
        remote(5, packed.at[1, :, top, :], sides.at[0, :, far, :], (up, right)),
        remote(6, packed.at[0, :, bottom, :], sides.at[1, :, pl.ds(0, HALF), :], (down, left)),
        remote(7, packed.at[1, :, bottom, :], sides.at[0, :, pl.ds(0, HALF), :], (down, right)),
    ]
    for copy in copies:
        copy.start()
    for load in loads[2:]:
        load.wait()
    for copy in copies:
        copy.wait()

    def smooth(g, carry):
        edge = jnp.concatenate([sides[0, g], sides[1, g]], axis=1)
        edge = dot(jnp.concatenate([edge, edge], axis=1), strip_w[...])
        for s in range(0, fold, 2):
            terms = []
            for t in (s, s + 1):
                plane = ext[g * fold + t]
                across = dot(jnp.concatenate([plane, plane], axis=1), own_w[...])
                terms.append(split_value(across + edge[:, t * width : (t + 1) * width]))
            high = jnp.concatenate([terms[0][0], terms[1][0]], axis=1)
            low = jnp.concatenate([terms[0][1], terms[1][1]], axis=1)
            result = dot(band_w[:, : 2 * tall], jnp.concatenate([high, low], axis=0))
            result += dot(band_w[:, 2 * tall :], high)
            for t in (0, 1):
                start = pl.multiple_of((g * fold + s + t) * height, 8)
                filtered[pl.ds(start, height), :] = result[:, t * width : (t + 1) * width]
        return carry

    lax.fori_loop(0, groups, smooth, 0)

    def correlate(i, total):
        wide, both = [], []
        for t in range(2):
            row = 2 * i + t
            high, low = split_value(filtered[pl.ds(row, count, stride=height), :])
            pair = jnp.concatenate([high, low], axis=0)
            field[row] = pair
            wide.append(high)
            both.append(pair)
        return total + lax.dot_general(
            jnp.concatenate(wide, axis=1), jnp.concatenate(both, axis=1),
            (((1,), (1,)), ((), ())), preferred_element_type=F32)

    total = lax.fori_loop(0, height // 2, correlate, jnp.zeros((count, 2 * count), F32))
    out = pltpu.make_async_copy(field, field_hbm, out_sem)
    out.start()
    cross = total[:, count:]
    gram = total[:, :count] + (cross + cross.T)
    part = jnp.concatenate([gram[: count // 2], gram[count // 2 :]], axis=1)

    def reduce(part, size, me, slots, sends, recvs, device):
        slots[me] = part
        copies = []
        for k in range(1, size):
            copy = pltpu.make_async_remote_copy(
                src_ref=slots.at[me], dst_ref=slots.at[me], send_sem=sends.at[k], recv_sem=recvs.at[k],
                device_id=device(lax.rem(me + k, size)), device_id_type=MESH)
            copy.start()
            copies.append(copy)
        for copy in copies:
            copy.wait()
        total = slots[0]
        for k in range(1, size):
            total = total + slots[k]
        return total

    part = reduce(part, rows, me_r, slots_r, send_r, recv_r, lambda r: (r, me_c))
    part = reduce(part, cols, me_c, slots_c, send_c, recv_c, lambda c: (me_r, c))
    points = height * width * rows * cols
    gram_ref[...] = part * np.float32(1.0 / points)
    out.wait()


def factor(gram):
    size = gram.shape[0]
    row = lax.broadcasted_iota(jnp.int32, (size, 2 * size), 0)
    lane = lax.broadcasted_iota(jnp.int32, (size, 2 * size), 1)
    identity = (row == lane - size).astype(F32)
    state = jnp.concatenate([gram, jnp.zeros_like(gram)], axis=1) + identity
    done = []
    for k in range(0, size, 8):
        live = size - k
        index = lax.broadcasted_iota(jnp.int32, (live, 2 * size), 0)
        columns = [jnp.broadcast_to(state[:, k + j : k + j + 1], (live, 2 * size)) for j in range(8)]
        pivots = [state[j : j + 1, :] for j in range(8)]
        scales = []
        for j in range(8):
            pivot = columns[j][j : j + 1, :]
            inverse = 1.0 / pivot
            scaled = columns[j] * inverse
            for t in range(j + 1, 8):
                ratio = scaled[t : t + 1, :]
                columns[t] = columns[t] - columns[j] * ratio
                pivots[t] = pivots[t] - ratio * pivots[j]
            if live > 8:
                state = state - scaled * pivots[j]
            scales.append(pivots[j] * lax.rsqrt(pivot))
        done.append(jnp.concatenate(scales, axis=0))
        state = state[8:]
    done = jnp.concatenate(done, axis=0)
    keep = (lane >= size) | (lane >= row)
    return jnp.where(keep, done, 0.0)


def basis_kernel(chunk, gram_ref, field_hbm, q_hbm, r_ref, field, basis, load_sem, store_sem):
    height, _, width = field.shape
    count = r_ref.shape[0]
    load = pltpu.make_async_copy(field_hbm, field, load_sem)
    load.start()
    packed = gram_ref[...]
    gram = jnp.concatenate([packed[:, :count], packed[:, count:]], axis=0)
    both = factor(gram)
    r_ref[...] = both[:, :count]
    high, low = split_value(both[:, count:])
    twice = jnp.concatenate([high, high], axis=1)
    load.wait()
    stores = []
    for c in range(height // chunk):
        view = basis.at[c].reshape(count * chunk, width)
        for i in range(0, chunk, 2):
            row = c * chunk + i
            pair = jnp.concatenate([field[row], field[row + 1]], axis=1)
            result = dot(twice, pair) + dot(low, pair[:count])
            for t in range(2):
                view[pl.ds(i + t, count, stride=chunk), :] = result[:, t * width : (t + 1) * width]
        store = pltpu.make_async_copy(basis.at[c], q_hbm.at[:, pl.ds(c * chunk, chunk), :], store_sem.at[c])
        store.start()
        stores.append(store)
    for store in stores:
        store.wait()


def local(rows, cols, snapshots):
    count, height, width = snapshots.shape
    pick, own_w, strip_w, rows_w = constants(height, width)
    tall = height + 2 * HALF
    groups = count * HALF // width
    anywhere = pl.BlockSpec(memory_space=pl.ANY)
    vmem = pl.BlockSpec(memory_space=pltpu.VMEM)
    dma = pltpu.SemaphoreType.DMA
    half = (count // 2, 2 * count)
    field, gram = pl.pallas_call(
        functools.partial(filter_kernel, rows, cols),
        out_shape=(jax.ShapeDtypeStruct((height, 2 * count, width), BF16), jax.ShapeDtypeStruct(half, F32)),
        in_specs=[anywhere] * 5,
        out_specs=(anywhere, vmem),
        scratch_shapes=[
            pltpu.VMEM((count, tall, width), BF16),
            pltpu.VMEM((2, groups, tall, width), BF16),
            pltpu.VMEM((2, groups, height, width), BF16),
            pltpu.VMEM(pick.shape, BF16),
            pltpu.VMEM(own_w.shape, BF16),
            pltpu.VMEM(strip_w.shape, BF16),
            pltpu.VMEM(rows_w.shape, BF16),
            pltpu.VMEM((count * height, width), F32),
            pltpu.VMEM((height, 2 * count, width), BF16),
            pltpu.VMEM((rows,) + half, F32),
            pltpu.VMEM((cols,) + half, F32),
            dma((5,)), dma((8,)), dma((8,)), dma((rows,)), dma((rows,)), dma((cols,)), dma((cols,)), dma,
        ],
        compiler_params=pltpu.CompilerParams(
            collective_id=0, has_side_effects=True, vmem_limit_bytes=40 * 2**20),
    )(snapshots, jnp.asarray(pick), jnp.asarray(own_w), jnp.asarray(strip_w), jnp.asarray(rows_w))
    chunk = 24 if height % 24 == 0 else 8
    return pl.pallas_call(
        functools.partial(basis_kernel, chunk),
        out_shape=(jax.ShapeDtypeStruct(snapshots.shape, F32), jax.ShapeDtypeStruct((count, count), F32)),
        in_specs=[vmem, anywhere],
        out_specs=(anywhere, vmem),
        scratch_shapes=[
            pltpu.VMEM((height, 2 * count, width), BF16),
            pltpu.VMEM((height // chunk, count, chunk, width), F32),
            dma, dma((height // chunk,)),
        ],
        compiler_params=pltpu.CompilerParams(vmem_limit_bytes=40 * 2**20),
    )(gram, field)


def solution(mesh):
    rows, cols = mesh.shape["row"], mesh.shape["col"]
    return jax.shard_map(
        functools.partial(local, rows, cols),
        mesh=mesh,
        in_specs=(P(None, "row", "col"),),
        out_specs=(P(None, "row", "col"), P()),
        check_vma=False,
    )
```

time: 110 us -> 53.4 us (0.49)
  Pallas kernels: 0 us -> 47.1 us
  blocking collectives: 39.4 us -> 0 us
  matrix products: 22.2 us -> 0 us
  other arithmetic: 14.5 us -> 0 us
  waiting for transfers between devices: 13.6 us -> 0 us
  starting transfers between devices: 7.24 us -> 0 us
  local copies, waits for them, and re-layouts: 11.9 us -> 5.39 us
    pallas_call x0 -> x2, Pallas kernels: none -> 47.1 us  [the longest x1 42.5 us: local(): pl.pallas_call(functools.partial(filter_kernel, rows, cols), out_shape=(j...]
    psum x1 -> x0, blocking collectives: 39.4 us -> none  [local(): gram = lax.psum(local_gram, ('row', 'col'))]
    dot_general x3 -> x0, matrix products: 17.6 us -> none  [the longest x1 7.76 us: filter_columns(): jnp.einsum('src,cd->srd', field, band_matrix(width), precision=lax.Precis...]
    ppermute x4 -> x0, waiting for transfers between devices: 13.6 us -> none  [the longest x2 7.82 us: padded(): before = lax.ppermute(last, axis, up)]
    another operation x4 -> x0, other arithmetic: 11.4 us -> none  [the longest x3 6.52 us: local(): upper = jnp.linalg.cholesky(gram).T]
    ppermute x4 -> x0, starting transfers between devices: 7.24 us -> none  [the longest x2 5.69 us: padded(): after = lax.ppermute(initial, axis, down)]
    another operation x1 -> x0, matrix products: 4.61 us -> none  [local(): lax.linalg.triangular_solve(upper.T, flat_field, left_side=True, lower=True)]
    ppermute x2 -> x0, local copies, waits for them, and re-layouts: 3.48 us -> none  [the longest x1 1.77 us: padded(): before = lax.ppermute(last, axis, up)]
  transfers between devices with their start and end apart: 4 -> 0, of which waited for: 3 -> 0; matrix products, arithmetic and copies ran while one was open for 5% -> 0% of each run, Pallas kernels for 0% -> 0%
where the time goes in v1:
time: 53.4 us; the launch traced here: 53.1 us
  Pallas kernels  47.1 us (88%)
  local copies, waits for them, and re-layouts  5.39 us (10%)
  between operations  0.65 us (1%)
    pallas_call x1, Pallas kernels, local(): pl.pallas_call(functools.partial(filter_kernel, rows, cols), out_shape=(j...  42.5 us
    unnamed x10, local copies, waits for them, and re-layouts  5.39 us
    pallas_call x1, Pallas kernels, local(): pl.pallas_call(functools.partial(basis_kernel, chunk), out_shape=(jax.Sha...  4.53 us

profile of v1, /device:TPU:0, one launch (start us, length us, event | category | flops | bytes accessed | tf_op | source)
XLA Modules:
  0.0 53.1 jit_solution(10902974627395723496)
XLA Ops:
  0.6 0.0 copy-start
  0.6 1.4 %copy-done = bf16[64,96,128]{2,1,0:T(8,128)(2,1)S(1)} copy-done((bf16[64,96,128]{2,1,0:T(8,128)(2,1)S(1)}, bf16[64,96,128]{2,1,0:T(8,128)(2,1)}, u32[]{:S(2)}) %copy-start) | copy-done | bytes 1572888
  2.0 0.0 copy-start.1
  2.0 1.2 %copy-done.1 = bf16[512,1024]{1,0:T(8,128)(2,1)S(1)} copy-done((bf16[512,1024]{1,0:T(8,128)(2,1)S(1)}, bf16[512,1024]{1,0:T(8,128)(2,1)}, u32[]{:S(2)}) %copy-start.1) | copy-done | bytes 1048600
  3.3 0.0 copy-start.2
  3.3 1.0 %copy-done.2 = bf16[1024,256]{1,0:T(8,128)(2,1)S(1)} copy-done((bf16[1024,256]{1,0:T(8,128)(2,1)S(1)}, bf16[1024,256]{1,0:T(8,128)(2,1)}, u32[]{:S(2)}) %copy-start.2) | copy-done | bytes 524312
  4.3 0.0 copy-start.3
  4.3 0.9 %copy-done.3 = bf16[96,384]{1,0:T(8,128)(2,1)S(1)} copy-done((bf16[96,384]{1,0:T(8,128)(2,1)S(1)}, bf16[96,384]{1,0:T(8,128)(2,1)}, u32[]{:S(2)}) %copy-start.3) | copy-done | bytes 73752
  5.2 0.0 copy-start.4
  5.2 0.8 %copy-done.4 = bf16[256,128]{1,0:T(8,128)(2,1)S(1)} copy-done((bf16[256,128]{1,0:T(8,128)(2,1)S(1)}, bf16[256,128]{1,0:T(8,128)(2,1)}, u32[]{:S(2)}) %copy-start.4) | copy-done | bytes 65560
  6.0 42.5 %shard_map.68 = (bf16[96,128,128]{2,1,0:T(8,128)(2,1)S(1)}, f32[32,128]{1,0:T(8,128)S(1)}) custom-call(bf16[64,96,128]{2,1,0:T(8,128)(2,1)S(1)} %copy-done, bf16[1024,256]{1,0:T(8,128)(2,1)S(1)} %copy-done.2, bf16[256,128]{1,0:T(8,128)(2,1)S(1)} %copy-done.4, bf16[512,1024]{1,0:T(8,128)(2,1)S(1)} %copy-done.1, bf16[96,384]{1,0:T(8,128)(2,1)S(1)} %copy-done.3), custom_call_target="tpu_custom_call" | custom-call | tf_op jit(solution)/shard_map/pallas_call | solution.py:267
  48.6 4.5 %shard_map.69 = (f32[64,96,128]{2,1,0:T(8,128)}, f32[64,64]{1,0:T(8,128)}) custom-call(f32[32,128]{1,0:T(8,128)S(1)} %get-tuple-element.4.gram_ref, bf16[96,128,128]{2,1,0:T(8,128)(2,1)S(1)} %get-tuple-element.5.field_hbm), custom_call_target="tpu_custom_call" | custom-call | tf_op jit(solution)/shard_map/pallas_call | solution.py:290
Async XLA Ops:
  0.6 1.4 %copy-start = (bf16[64,96,128]{2,1,0:T(8,128)(2,1)S(1)}, bf16[64,96,128]{2,1,0:T(8,128)(2,1)}, u32[]{:S(2)}) copy-start(bf16[64,96,128]{2,1,0:T(8,128)(2,1)} %x_ref.1) | copy-start | bytes 4718596
  2.0 1.2 %copy-start.1 = (bf16[512,1024]{1,0:T(8,128)(2,1)S(1)}, bf16[512,1024]{1,0:T(8,128)(2,1)}, u32[]{:S(2)}) copy-start(bf16[512,1024]{1,0:T(8,128)(2,1)} %constant.10.clone.strip_hbm) | copy-start | bytes 3145732
  3.3 1.0 %copy-start.2 = (bf16[1024,256]{1,0:T(8,128)(2,1)S(1)}, bf16[1024,256]{1,0:T(8,128)(2,1)}, u32[]{:S(2)}) copy-start(bf16[1024,256]{1,0:T(8,128)(2,1)} %constant.8.clone.pick_hbm) | copy-start | bytes 1572868
  4.3 0.9 %copy-start.3 = (bf16[96,384]{1,0:T(8,128)(2,1)S(1)}, bf16[96,384]{1,0:T(8,128)(2,1)}, u32[]{:S(2)}) copy-start(bf16[96,384]{1,0:T(8,128)(2,1)} %constant.11.clone.band_hbm) | copy-start | bytes 221188
  5.2 0.8 %copy-start.4 = (bf16[256,128]{1,0:T(8,128)(2,1)S(1)}, bf16[256,128]{1,0:T(8,128)(2,1)}, u32[]{:S(2)}) copy-start(bf16[256,128]{1,0:T(8,128)(2,1)} %constant.9.clone.own_hbm) | copy-start | bytes 196612

commit v2 on v1

--- a/solution.py
+++ b/solution.py
@@ -38,23 +38,19 @@
 def constants(height, width):
     fold = width // HALF
     across = band(width)
-    own = across[HALF : HALF + width]
-    left, right = across[:HALF], across[HALF + width :]
-    own_w = np.concatenate(split_terms(own), axis=0)
-    strip = np.zeros((2, fold, HALF, fold, width), np.float32)
-    for s in range(fold):
-        strip[0, s, :, s] = left
-        strip[1, s, :, s] = right
-    strip_w = np.concatenate(split_terms(strip.reshape(2 * width, fold * width)), axis=0)
+    joint = np.zeros((fold, 2 * width, width), np.float32)
     pick = np.zeros((fold, width, 2, fold, HALF), np.float32)
     for s in range(fold):
+        joint[s, :width] = across[HALF : HALF + width]
+        joint[s, width + s * HALF : width + (s + 1) * HALF] = across[:HALF]
+        joint[s, width + (s ^ 1) * HALF : width + ((s ^ 1) + 1) * HALF] = across[HALF + width :]
         for c in range(HALF):
-            pick[s, c, 0, s, c] = 1.0
-            pick[s, width - HALF + c, 1, s, c] = 1.0
+            pick[s, width - HALF + c, 0, s, c] = 1.0
+            pick[s, c, 1, s ^ 1, c] = 1.0
     pick = pick.reshape(fold * width, 2 * width).astype(ml_dtypes.bfloat16)
-    high, low = split_terms(np.ascontiguousarray(band(height).T))
-    rows_w = np.concatenate([high, high, low], axis=1)
-    return pick, own_w, strip_w, rows_w
+    joint = np.concatenate(split_terms(joint), axis=2)
+    rows_w = np.concatenate(split_terms(np.ascontiguousarray(band(height).T)), axis=0)
+    return pick, joint, rows_w
 
 
 def split_value(value):
@@ -66,13 +62,14 @@
     return jnp.dot(a, b, preferred_element_type=F32)
 
 
-def filter_kernel(rows, cols, x_ref, pick_hbm, own_hbm, strip_hbm, band_hbm, field_hbm, gram_ref,
-                  ext, sides, packed, pick, own_w, strip_w, band_w, filtered, field, slots_r, slots_c,
-                  load_sem, send_sem, recv_sem, send_r, recv_r, send_c, recv_c, out_sem):
+def filter_kernel(rows, cols, x_ref, pick_hbm, joint_hbm, band_hbm, field_hbm, gram_ref,
+                  ext, sides, packed, pick, joint, band_w, own_h, own_l, edge_h, edge_l, filtered, field,
+                  slots_r, slots_c, load_sem, send_sem, recv_sem, send_r, recv_r, send_c, recv_c, out_sem):
     count, height, width = x_ref.shape
-    tall = height + 2 * HALF
     fold = width // HALF
     groups = count // fold
+    part_groups = groups // 2
+    pitch = filtered.shape[0] // count
     me_r, me_c = lax.axis_index("row"), lax.axis_index("col")
     up, down = lax.rem(me_r + rows - 1, rows), lax.rem(me_r + 1, rows)
     left, right = lax.rem(me_c + cols - 1, cols), lax.rem(me_c + 1, cols)
@@ -81,9 +78,8 @@
     loads = [
         pltpu.make_async_copy(x_ref, ext.at[:, body, :], load_sem.at[0]),
         pltpu.make_async_copy(pick_hbm, pick, load_sem.at[1]),
-        pltpu.make_async_copy(own_hbm, own_w, load_sem.at[2]),
-        pltpu.make_async_copy(strip_hbm, strip_w, load_sem.at[3]),
-        pltpu.make_async_copy(band_hbm, band_w, load_sem.at[4]),
+        pltpu.make_async_copy(band_hbm, band_w, load_sem.at[2]),
+        pltpu.make_async_copy(joint_hbm, joint, load_sem.at[3]),
     ]
     for load in loads:
         load.start()
@@ -95,19 +91,6 @@
     for friend in friends:
         pl.semaphore_signal(barrier, inc=1, device_id=friend, device_id_type=MESH)
 
-    loads[0].wait()
-    loads[1].wait()
-
-    def pack(g, carry):
-        planes = [ext[g * fold + s, HALF : HALF + height, :] for s in range(fold)]
-        strips = dot(jnp.concatenate(planes, axis=1), pick[...]).astype(BF16)
-        packed[0, g] = strips[:, :width]
-        packed[1, g] = strips[:, width:]
-        return carry
-
-    lax.fori_loop(0, groups, pack, 0)
-    pl.semaphore_wait(barrier, len(friends))
-
     top, bottom = pl.ds(0, HALF), pl.ds(height - HALF, HALF)
     far = pl.ds(HALF + height, HALF)
 
@@ -116,48 +99,106 @@
             src_ref=src, dst_ref=dst, send_sem=send_sem.at[index], recv_sem=recv_sem.at[index],
             device_id=device, device_id_type=MESH)
 
-    copies = [
-        remote(0, packed.at[0], sides.at[1, :, body, :], (me_r, left)),
-        remote(1, packed.at[1], sides.at[0, :, body, :], (me_r, right)),
-        remote(2, x_ref.at[:, top, :], ext.at[:, far, :], (up, me_c)),
-        remote(3, x_ref.at[:, bottom, :], ext.at[:, pl.ds(0, HALF), :], (down, me_c)),
-        remote(4, packed.at[0, :, top, :], sides.at[1, :, far, :], (up, left)),
-        remote(5, packed.at[1, :, top, :], sides.at[0, :, far, :], (up, right)),
-        remote(6, packed.at[0, :, bottom, :], sides.at[1, :, pl.ds(0, HALF), :], (down, left)),
-        remote(7, packed.at[1, :, bottom, :], sides.at[0, :, pl.ds(0, HALF), :], (down, right)),
+    def strips(h):
+        part = pl.ds(h * part_groups, part_groups)
+        return [
+            remote(2 * h, packed.at[0, part], sides.at[0, part, body, :], (me_r, right)),
+            remote(2 * h + 1, packed.at[1, part], sides.at[1, part, body, :], (me_r, left)),
+        ]
+
+    edges = [
+        remote(4, x_ref.at[:, top, :], ext.at[:, far, :], (up, me_c)),
+        remote(5, x_ref.at[:, bottom, :], ext.at[:, pl.ds(0, HALF), :], (down, me_c)),
     ]
-    for copy in copies:
+    corners = [
+        remote(6, packed.at[0, :, top, :], sides.at[0, :, far, :], (up, right)),
+        remote(7, packed.at[1, :, top, :], sides.at[1, :, far, :], (up, left)),
+        remote(8, packed.at[0, :, bottom, :], sides.at[0, :, pl.ds(0, HALF), :], (down, right)),
+        remote(9, packed.at[1, :, bottom, :], sides.at[1, :, pl.ds(0, HALF), :], (down, left)),
+    ]
+
+    def pack(h):
+        planes = []
+        for s in range(fold):
+            first = h * part_groups * fold + s
+            planes.append(jnp.concatenate(
+                [ext[first + g * fold, HALF : HALF + height, :] for g in range(part_groups)], axis=0))
+        chosen = dot(jnp.concatenate(planes, axis=1), pick[...]).astype(BF16)
+        for g in range(part_groups):
+            lines = chosen[g * height : (g + 1) * height]
+            packed[0, h * part_groups + g] = lines[:, :width]
+            packed[1, h * part_groups + g] = lines[:, width:]
+
+    loads[0].wait()
+    loads[1].wait()
+    pack(0)
+    pl.semaphore_wait(barrier, len(friends))
+    for copy in strips(0) + edges:
         copy.start()
-    for load in loads[2:]:
-        load.wait()
-    for copy in copies:
+    pack(1)
+    for copy in strips(1) + corners:
+        copy.start()
+
+    loads[2].wait()
+    for copy in edges:
         copy.wait()
 
-    def smooth(g, carry):
-        edge = jnp.concatenate([sides[0, g], sides[1, g]], axis=1)
-        edge = dot(jnp.concatenate([edge, edge], axis=1), strip_w[...])
+    def down_rows(pair):
+        both = dot(band_w[...], pair)
+        return both[:height] + both[height:]
+
+    def own_rows(g, carry):
+        start = pl.ds(pl.multiple_of(g * height, 16), height)
         for s in range(0, fold, 2):
-            terms = []
-            for t in (s, s + 1):
-                plane = ext[g * fold + t]
-                across = dot(jnp.concatenate([plane, plane], axis=1), own_w[...])
-                terms.append(split_value(across + edge[:, t * width : (t + 1) * width]))
-            high = jnp.concatenate([terms[0][0], terms[1][0]], axis=1)
-            low = jnp.concatenate([terms[0][1], terms[1][1]], axis=1)
-            result = dot(band_w[:, : 2 * tall], jnp.concatenate([high, low], axis=0))
-            result += dot(band_w[:, 2 * tall :], high)
+            n = g * fold + s
+            result = down_rows(jnp.concatenate([ext[n], ext[n + 1]], axis=1))
             for t in (0, 1):
-                start = pl.multiple_of((g * fold + s + t) * height, 8)
-                filtered[pl.ds(start, height), :] = result[:, t * width : (t + 1) * width]
+                high, low = split_value(result[:, t * width : (t + 1) * width])
+                own_h[s + t, start, :] = high
+                own_l[s + t, start, :] = low
         return carry
 
-    lax.fori_loop(0, groups, smooth, 0)
+    lax.fori_loop(0, groups, own_rows, 0)
+    loads[3].wait()
+    lane = lax.broadcasted_iota(jnp.int32, (height, width), 1)
+    even = lax.rem(lane // HALF, 2) == 0
+
+    for h in range(2):
+        for copy in strips(h) + (corners if h == 0 else []):
+            copy.wait()
+
+        def edge_rows(i, carry):
+            g = h * part_groups + i
+            result = down_rows(jnp.concatenate([sides[0, g], sides[1, g]], axis=1))
+            before, after = result[:, :width], result[:, width:]
+            start = pl.ds(pl.multiple_of(g * height, 16), height)
+            for t, plane in enumerate((jnp.where(even, before, after), jnp.where(even, after, before))):
+                high, low = split_value(plane)
+                edge_h[t, start, :] = high
+                edge_l[t, start, :] = low
+            return carry
+
+        lax.fori_loop(0, part_groups, edge_rows, 0)
+        block = pl.ds(h * part_groups * height, part_groups * height)
+
+        def columns(s, carry):
+            parity = lax.rem(s, 2)
+            result = dot(jnp.concatenate([own_h[s, block, :], edge_h[parity, block, :]], axis=1), joint[s])
+            extra = dot(jnp.concatenate([own_l[s, block, :], edge_l[parity, block, :]], axis=1),
+                        joint[s, :, :width])
+            result = result[:, :width] + (result[:, width:] + extra)
+            for g in range(part_groups):
+                start = pl.multiple_of(((h * part_groups + g) * fold + s) * pitch, 8)
+                filtered[pl.ds(start, height), :] = result[g * height : (g + 1) * height]
+            return carry
+
+        lax.fori_loop(0, fold, columns, 0)
 
     def correlate(i, total):
         wide, both = [], []
         for t in range(2):
             row = 2 * i + t
-            high, low = split_value(filtered[pl.ds(row, count, stride=height), :])
+            high, low = split_value(filtered[pl.ds(row, count, stride=pitch), :])
             pair = jnp.concatenate([high, low], axis=0)
             field[row] = pair
             wide.append(high)
@@ -257,35 +298,41 @@
 
 def local(rows, cols, snapshots):
     count, height, width = snapshots.shape
-    pick, own_w, strip_w, rows_w = constants(height, width)
+    pick, joint, rows_w = constants(height, width)
     tall = height + 2 * HALF
-    groups = count * HALF // width
+    fold = width // HALF
+    groups = count // fold
+    pitch = height + 8 if height % 16 == 0 else height
     anywhere = pl.BlockSpec(memory_space=pl.ANY)
+    hbm = pl.BlockSpec(memory_space=pltpu.HBM)
     vmem = pl.BlockSpec(memory_space=pltpu.VMEM)
     dma = pltpu.SemaphoreType.DMA
     half = (count // 2, 2 * count)
     field, gram = pl.pallas_call(
         functools.partial(filter_kernel, rows, cols),
         out_shape=(jax.ShapeDtypeStruct((height, 2 * count, width), BF16), jax.ShapeDtypeStruct(half, F32)),
-        in_specs=[anywhere] * 5,
+        in_specs=[hbm] * 4,
         out_specs=(anywhere, vmem),
         scratch_shapes=[
             pltpu.VMEM((count, tall, width), BF16),
             pltpu.VMEM((2, groups, tall, width), BF16),
             pltpu.VMEM((2, groups, height, width), BF16),
             pltpu.VMEM(pick.shape, BF16),
-            pltpu.VMEM(own_w.shape, BF16),
-            pltpu.VMEM(strip_w.shape, BF16),
+            pltpu.VMEM(joint.shape, BF16),
             pltpu.VMEM(rows_w.shape, BF16),
-            pltpu.VMEM((count * height, width), F32),
+            pltpu.VMEM((fold, groups * height, width), BF16),
+            pltpu.VMEM((fold, groups * height, width), BF16),
+            pltpu.VMEM((2, groups * height, width), BF16),
+            pltpu.VMEM((2, groups * height, width), BF16),
+            pltpu.VMEM((count * pitch, width), F32),
             pltpu.VMEM((height, 2 * count, width), BF16),
             pltpu.VMEM((rows,) + half, F32),
             pltpu.VMEM((cols,) + half, F32),
-            dma((5,)), dma((8,)), dma((8,)), dma((rows,)), dma((rows,)), dma((cols,)), dma((cols,)), dma,
+            dma((4,)), dma((10,)), dma((10,)), dma((rows,)), dma((rows,)), dma((cols,)), dma((cols,)), dma,
         ],
         compiler_params=pltpu.CompilerParams(
-            collective_id=0, has_side_effects=True, vmem_limit_bytes=40 * 2**20),
-    )(snapshots, jnp.asarray(pick), jnp.asarray(own_w), jnp.asarray(strip_w), jnp.asarray(rows_w))
+            collective_id=0, has_side_effects=True, vmem_limit_bytes=63 * 2**20),
+    )(snapshots, jnp.asarray(pick), jnp.asarray(joint), jnp.asarray(rows_w))
     chunk = 24 if height % 24 == 0 else 8
     return pl.pallas_call(
         functools.partial(basis_kernel, chunk),
@@ -297,7 +344,7 @@
             pltpu.VMEM((height // chunk, count, chunk, width), F32),
             dma, dma((height // chunk,)),
         ],
-        compiler_params=pltpu.CompilerParams(vmem_limit_bytes=40 * 2**20),
+        compiler_params=pltpu.CompilerParams(vmem_limit_bytes=63 * 2**20),
     )(gram, field)
 
 

time: 53.4 us -> 47 us (0.88)
  local copies, waits for them, and re-layouts: 5.39 us -> 0 us
  Pallas kernels: 47.1 us -> 46.1 us
    unnamed x10 -> x0, local copies, waits for them, and re-layouts: 5.39 us -> none
    pallas_call x1, Pallas kernels: 42.5 us -> 40.8 us  [local(): pl.pallas_call(functools.partial(filter_kernel, rows, cols), out_shape=(j...]
    pallas_call x1, Pallas kernels: 4.53 us -> 5.33 us  [local(): pl.pallas_call(functools.partial(basis_kernel, chunk), out_shape=(jax.Sha...]
where the time goes in v2:
time: 47 us; the launch traced here: 46.8 us
  Pallas kernels  46.1 us (98%)
  between operations  0.64 us (1%)
    pallas_call x1, Pallas kernels, local(): pl.pallas_call(functools.partial(filter_kernel, rows, cols), out_shape=(j...  40.8 us
    pallas_call x1, Pallas kernels, local(): pl.pallas_call(functools.partial(basis_kernel, chunk), out_shape=(jax.Sha...  5.33 us

profile of v2, /device:TPU:0, one launch (start us, length us, event | category | flops | bytes accessed | tf_op | source)
XLA Modules:
  0.0 46.8 jit_solution(8268579717308599000)
XLA Ops:
  0.6 40.8 %shard_map.59 = (bf16[96,128,128]{2,1,0:T(8,128)(2,1)}, f32[32,128]{1,0:T(8,128)}) custom-call(bf16[64,96,128]{2,1,0:T(8,128)(2,1)} %x_ref.1, bf16[1024,256]{1,0:T(8,128)(2,1)} %constant.6.clone.pick_hbm, bf16[8,256,256]{2,1,0:T(8,128)(2,1)} %constant.7.clone.joint_hbm, bf16[192,128]{1,0:T(8,128)(2,1)} %constant.8.clone.band_hbm), custom_call_target="tpu_custom_call" | custom-call | tf_op jit(solution)/shard_map/pallas_call | solution.py:311
  41.5 5.3 %shard_map.60 = (f32[64,96,128]{2,1,0:T(8,128)}, f32[64,64]{1,0:T(8,128)}) custom-call(f32[32,128]{1,0:T(8,128)} %get-tuple-element.4.gram_ref, bf16[96,128,128]{2,1,0:T(8,128)(2,1)} %get-tuple-element.5.field_hbm), custom_call_target="tpu_custom_call" | custom-call | tf_op jit(solution)/shard_map/pallas_call | solution.py:337

commit v3 on v2

--- a/solution.py
+++ b/solution.py
@@ -64,11 +64,13 @@
 
 def filter_kernel(rows, cols, x_ref, pick_hbm, joint_hbm, band_hbm, field_hbm, gram_ref,
                   ext, sides, packed, pick, joint, band_w, own_h, own_l, edge_h, edge_l, filtered, field,
-                  slots_r, slots_c, load_sem, send_sem, recv_sem, send_r, recv_r, send_c, recv_c, out_sem):
+                  stage, slots_r, slots_c, gathered, load_sem, send_sem, recv_sem, send_r, recv_r, send_c, recv_c,
+                  send_g, recv_g, out_sem):
     count, height, width = x_ref.shape
     fold = width // HALF
     groups = count // fold
-    part_groups = groups // 2
+    parts = 4 if groups % 4 == 0 else 1
+    part_groups = groups // parts
     pitch = filtered.shape[0] // count
     me_r, me_c = lax.axis_index("row"), lax.axis_index("col")
     up, down = lax.rem(me_r + rows - 1, rows), lax.rem(me_r + 1, rows)
@@ -81,13 +83,12 @@
         pltpu.make_async_copy(band_hbm, band_w, load_sem.at[2]),
         pltpu.make_async_copy(joint_hbm, joint, load_sem.at[3]),
     ]
-    for load in loads:
+    for load in loads[:2]:
         load.start()
 
     barrier = pltpu.get_barrier_semaphore()
     friends = [(lax.rem(me_r + k, rows), me_c) for k in range(1, rows)]
     friends += [(me_r, lax.rem(me_c + k, cols)) for k in range(1, cols)]
-    friends += [(up, left), (up, right), (down, left), (down, right)]
     for friend in friends:
         pl.semaphore_signal(barrier, inc=1, device_id=friend, device_id_type=MESH)
 
@@ -107,15 +108,18 @@
         ]
 
     edges = [
-        remote(4, x_ref.at[:, top, :], ext.at[:, far, :], (up, me_c)),
-        remote(5, x_ref.at[:, bottom, :], ext.at[:, pl.ds(0, HALF), :], (down, me_c)),
+        remote(2 * parts, x_ref.at[:, top, :], ext.at[:, far, :], (up, me_c)),
+        remote(2 * parts + 1, x_ref.at[:, bottom, :], ext.at[:, pl.ds(0, HALF), :], (down, me_c)),
     ]
-    corners = [
-        remote(6, packed.at[0, :, top, :], sides.at[0, :, far, :], (up, right)),
-        remote(7, packed.at[1, :, top, :], sides.at[1, :, far, :], (up, left)),
-        remote(8, packed.at[0, :, bottom, :], sides.at[0, :, pl.ds(0, HALF), :], (down, right)),
-        remote(9, packed.at[1, :, bottom, :], sides.at[1, :, pl.ds(0, HALF), :], (down, left)),
-    ]
+
+    def corners(h):
+        part = pl.ds(h * part_groups, part_groups)
+        first = 2 * parts + 2 + 2 * h
+        return [
+            remote(first, sides.at[:, part, pl.ds(HALF, HALF), :], sides.at[:, part, far, :], (up, me_c)),
+            remote(first + 1, sides.at[:, part, pl.ds(height, HALF), :], sides.at[:, part, pl.ds(0, HALF), :],
+                   (down, me_c)),
+        ]
 
     def pack(h):
         planes = []
@@ -135,9 +139,12 @@
     pl.semaphore_wait(barrier, len(friends))
     for copy in strips(0) + edges:
         copy.start()
-    pack(1)
-    for copy in strips(1) + corners:
-        copy.start()
+    for load in loads[2:]:
+        load.start()
+    for h in range(1, parts):
+        pack(h)
+        for copy in strips(h):
+            copy.start()
 
     loads[2].wait()
     for copy in edges:
@@ -147,9 +154,10 @@
         both = dot(band_w[...], pair)
         return both[:height] + both[height:]
 
-    def own_rows(g, carry):
-        start = pl.ds(pl.multiple_of(g * height, 16), height)
-        for s in range(0, fold, 2):
+    def own_rows(i, carry):
+        for j in range(0, 2 * fold, 2):
+            g, s = 2 * i + j // fold, j % fold
+            start = pl.ds(pl.multiple_of(g * height, 16), height)
             n = g * fold + s
             result = down_rows(jnp.concatenate([ext[n], ext[n + 1]], axis=1))
             for t in (0, 1):
@@ -158,46 +166,53 @@
                 own_l[s + t, start, :] = low
         return carry
 
-    lax.fori_loop(0, groups, own_rows, 0)
+    lax.fori_loop(0, groups // 2, own_rows, 0)
     loads[3].wait()
     lane = lax.broadcasted_iota(jnp.int32, (height, width), 1)
     even = lax.rem(lane // HALF, 2) == 0
 
-    for h in range(2):
-        for copy in strips(h) + (corners if h == 0 else []):
+    def finish(h):
+        for copy in corners(h):
             copy.wait()
-
-        def edge_rows(i, carry):
-            g = h * part_groups + i
+        for g in range(h * part_groups, (h + 1) * part_groups):
             result = down_rows(jnp.concatenate([sides[0, g], sides[1, g]], axis=1))
             before, after = result[:, :width], result[:, width:]
-            start = pl.ds(pl.multiple_of(g * height, 16), height)
+            start = pl.ds(g * height, height)
             for t, plane in enumerate((jnp.where(even, before, after), jnp.where(even, after, before))):
                 high, low = split_value(plane)
                 edge_h[t, start, :] = high
                 edge_l[t, start, :] = low
+        block = pl.ds(h * part_groups * height, part_groups * height)
+
+        def columns(i, carry):
+            for parity in range(2):
+                s = 2 * i + parity
+                result = dot(jnp.concatenate([own_h[s, block, :], edge_h[parity, block, :]], axis=1), joint[s])
+                extra = dot(jnp.concatenate([own_l[s, block, :], edge_l[parity, block, :]], axis=1),
+                            joint[s, :, :width])
+                result = result[:, :width] + (result[:, width:] + extra)
+                for g in range(part_groups):
+                    start = pl.multiple_of(((h * part_groups + g) * fold + s) * pitch, 8)
+                    filtered[pl.ds(start, height), :] = result[g * height : (g + 1) * height]
             return carry
 
-        lax.fori_loop(0, part_groups, edge_rows, 0)
-        block = pl.ds(h * part_groups * height, part_groups * height)
-
-        def columns(s, carry):
-            parity = lax.rem(s, 2)
-            result = dot(jnp.concatenate([own_h[s, block, :], edge_h[parity, block, :]], axis=1), joint[s])
-            extra = dot(jnp.concatenate([own_l[s, block, :], edge_l[parity, block, :]], axis=1),
-                        joint[s, :, :width])
-            result = result[:, :width] + (result[:, width:] + extra)
-            for g in range(part_groups):
-                start = pl.multiple_of(((h * part_groups + g) * fold + s) * pitch, 8)
-                filtered[pl.ds(start, height), :] = result[g * height : (g + 1) * height]
-            return carry
-
-        lax.fori_loop(0, fold, columns, 0)
+        lax.fori_loop(0, fold // 2, columns, 0)
+
+    for h in range(parts):
+        for copy in strips(h):
+            copy.wait()
+        for copy in corners(h):
+            copy.start()
+        if h > 0:
+            finish(h - 1)
+    finish(parts - 1)
+
+    step = 16 if height % 16 == 0 else 2
 
     def correlate(i, total):
         wide, both = [], []
-        for t in range(2):
-            row = 2 * i + t
+        for t in range(step):
+            row = step * i + t
             high, low = split_value(filtered[pl.ds(row, count, stride=pitch), :])
             pair = jnp.concatenate([high, low], axis=0)
             field[row] = pair
@@ -207,31 +222,46 @@
             jnp.concatenate(wide, axis=1), jnp.concatenate(both, axis=1),
             (((1,), (1,)), ((), ())), preferred_element_type=F32)
 
-    total = lax.fori_loop(0, height // 2, correlate, jnp.zeros((count, 2 * count), F32))
+    total = lax.fori_loop(0, height // step, correlate, jnp.zeros((count, 2 * count), F32))
     out = pltpu.make_async_copy(field, field_hbm, out_sem)
     out.start()
     cross = total[:, count:]
     gram = total[:, :count] + (cross + cross.T)
     part = jnp.concatenate([gram[: count // 2], gram[count // 2 :]], axis=1)
 
-    def reduce(part, size, me, slots, sends, recvs, device):
-        slots[me] = part
+    def exchange(size, me, source, slots, sends, recvs, device):
         copies = []
         for k in range(1, size):
+            other = lax.rem(me + k, size)
             copy = pltpu.make_async_remote_copy(
-                src_ref=slots.at[me], dst_ref=slots.at[me], send_sem=sends.at[k], recv_sem=recvs.at[k],
-                device_id=device(lax.rem(me + k, size)), device_id_type=MESH)
+                src_ref=source(other), dst_ref=slots.at[me], send_sem=sends.at[k], recv_sem=recvs.at[k],
+                device_id=device(other), device_id_type=MESH)
             copy.start()
             copies.append(copy)
         for copy in copies:
             copy.wait()
+
+    def added(slots, size):
         total = slots[0]
         for k in range(1, size):
             total = total + slots[k]
         return total
 
-    part = reduce(part, rows, me_r, slots_r, send_r, recv_r, lambda r: (r, me_c))
-    part = reduce(part, cols, me_c, slots_c, send_c, recv_c, lambda c: (me_r, c))
+    in_row, in_col = (lambda r: (r, me_c)), (lambda c: (me_r, c))
+    scatter = stage.shape[0] == rows
+    lines = stage.shape[1]
+    for r in range(stage.shape[0]):
+        stage[r] = part[r * lines : (r + 1) * lines]
+    mine = me_r if scatter else 0
+    slots_r[me_r] = stage[mine]
+    exchange(rows, me_r, lambda r: stage.at[r if scatter else 0], slots_r, send_r, recv_r, in_row)
+    slots_c[me_c] = added(slots_r, rows)
+    exchange(cols, me_c, lambda c: slots_c.at[me_c], slots_c, send_c, recv_c, in_col)
+    part = added(slots_c, cols)
+    if scatter:
+        gathered[me_r] = part
+        exchange(rows, me_r, lambda r: gathered.at[me_r], gathered, send_g, recv_g, in_row)
+        part = jnp.concatenate([gathered[r] for r in range(rows)], axis=0)
     points = height * width * rows * cols
     gram_ref[...] = part * np.float32(1.0 / points)
     out.wait()
@@ -279,6 +309,8 @@
     r_ref[...] = both[:, :count]
     high, low = split_value(both[:, count:])
     twice = jnp.concatenate([high, high], axis=1)
+    once = jnp.concatenate([low, jnp.zeros_like(low)], axis=1)
+    inverse = jnp.concatenate([twice, once], axis=0)
     load.wait()
     stores = []
     for c in range(height // chunk):
@@ -286,7 +318,8 @@
         for i in range(0, chunk, 2):
             row = c * chunk + i
             pair = jnp.concatenate([field[row], field[row + 1]], axis=1)
-            result = dot(twice, pair) + dot(low, pair[:count])
+            result = dot(inverse, pair)
+            result = result[:count] + result[count:]
             for t in range(2):
                 view[pl.ds(i + t, count, stride=chunk), :] = result[:, t * width : (t + 1) * width]
         store = pltpu.make_async_copy(basis.at[c], q_hbm.at[:, pl.ds(c * chunk, chunk), :], store_sem.at[c])
@@ -308,6 +341,8 @@
     vmem = pl.BlockSpec(memory_space=pltpu.VMEM)
     dma = pltpu.SemaphoreType.DMA
     half = (count // 2, 2 * count)
+    pieces = rows if half[0] % (8 * rows) == 0 else 1
+    piece = (half[0] // pieces, half[1])
     field, gram = pl.pallas_call(
         functools.partial(filter_kernel, rows, cols),
         out_shape=(jax.ShapeDtypeStruct((height, 2 * count, width), BF16), jax.ShapeDtypeStruct(half, F32)),
@@ -326,9 +361,12 @@
             pltpu.VMEM((2, groups * height, width), BF16),
             pltpu.VMEM((count * pitch, width), F32),
             pltpu.VMEM((height, 2 * count, width), BF16),
-            pltpu.VMEM((rows,) + half, F32),
-            pltpu.VMEM((cols,) + half, F32),
-            dma((4,)), dma((10,)), dma((10,)), dma((rows,)), dma((rows,)), dma((cols,)), dma((cols,)), dma,
+            pltpu.VMEM((pieces,) + piece, F32),
+            pltpu.VMEM((rows,) + piece, F32),
+            pltpu.VMEM((cols,) + piece, F32),
+            pltpu.VMEM((rows,) + piece, F32),
+            dma((4,)), dma((18,)), dma((18,)), dma((rows,)), dma((rows,)), dma((cols,)), dma((cols,)),
+            dma((rows,)), dma((rows,)), dma,
         ],
         compiler_params=pltpu.CompilerParams(
             collective_id=0, has_side_effects=True, vmem_limit_bytes=63 * 2**20),

time: 47 us -> 42.2 us (0.90)
  Pallas kernels: 46.1 us -> 41.3 us
    pallas_call x1, Pallas kernels: 40.8 us -> 36 us  [local(): pl.pallas_call(functools.partial(filter_kernel, rows, cols), out_shape=(j...]
where the time goes in v3:
time: 42.2 us; the launch traced here: 42 us
  Pallas kernels  41.3 us (98%)
  between operations  0.64 us (2%)
    pallas_call x1, Pallas kernels, local(): pl.pallas_call(functools.partial(filter_kernel, rows, cols), out_shape=(j...  36 us
    pallas_call x1, Pallas kernels, local(): pl.pallas_call(functools.partial(basis_kernel, chunk), out_shape=(jax.Sha...  5.28 us

profile of v3, /device:TPU:0, one launch (start us, length us, event | category | flops | bytes accessed | tf_op | source)
XLA Modules:
  0.0 42.0 jit_solution(11608474107264397309)
XLA Ops:
  0.6 36.0 %shard_map.59 = (bf16[96,128,128]{2,1,0:T(8,128)(2,1)}, f32[32,128]{1,0:T(8,128)}) custom-call(bf16[64,96,128]{2,1,0:T(8,128)(2,1)} %x_ref.1, bf16[1024,256]{1,0:T(8,128)(2,1)} %constant.6.clone.pick_hbm, bf16[8,256,256]{2,1,0:T(8,128)(2,1)} %constant.7.clone.joint_hbm, bf16[192,128]{1,0:T(8,128)(2,1)} %constant.8.clone.band_hbm), custom_call_target="tpu_custom_call" | custom-call | tf_op jit(solution)/shard_map/pallas_call | solution.py:346
  36.7 5.3 %shard_map.60 = (f32[64,96,128]{2,1,0:T(8,128)}, f32[64,64]{1,0:T(8,128)}) custom-call(f32[32,128]{1,0:T(8,128)} %get-tuple-element.4.gram_ref, bf16[96,128,128]{2,1,0:T(8,128)(2,1)} %get-tuple-element.5.field_hbm), custom_call_target="tpu_custom_call" | custom-call | tf_op jit(solution)/shard_map/pallas_call | solution.py:375

commit v4 on v3

--- a/solution.py
+++ b/solution.py
@@ -69,8 +69,8 @@
     count, height, width = x_ref.shape
     fold = width // HALF
     groups = count // fold
-    parts = 4 if groups % 4 == 0 else 1
-    part_groups = groups // parts
+    part_groups = groups // 2
+    parts = groups // 2
     pitch = filtered.shape[0] // count
     me_r, me_c = lax.axis_index("row"), lax.axis_index("col")
     up, down = lax.rem(me_r + rows - 1, rows), lax.rem(me_r + 1, rows)
@@ -83,12 +83,13 @@
         pltpu.make_async_copy(band_hbm, band_w, load_sem.at[2]),
         pltpu.make_async_copy(joint_hbm, joint, load_sem.at[3]),
     ]
-    for load in loads[:2]:
+    for load in loads:
         load.start()
 
     barrier = pltpu.get_barrier_semaphore()
     friends = [(lax.rem(me_r + k, rows), me_c) for k in range(1, rows)]
     friends += [(me_r, lax.rem(me_c + k, cols)) for k in range(1, cols)]
+    friends += [(up, left), (up, right), (down, left), (down, right)]
     for friend in friends:
         pl.semaphore_signal(barrier, inc=1, device_id=friend, device_id_type=MESH)
 
@@ -107,18 +108,22 @@
             remote(2 * h + 1, packed.at[1, part], sides.at[1, part, body, :], (me_r, left)),
         ]
 
-    edges = [
-        remote(2 * parts, x_ref.at[:, top, :], ext.at[:, far, :], (up, me_c)),
-        remote(2 * parts + 1, x_ref.at[:, bottom, :], ext.at[:, pl.ds(0, HALF), :], (down, me_c)),
-    ]
+    def edges(i):
+        part = pl.ds(i * (count // parts), count // parts)
+        first = 14 + 2 * i
+        return [
+            remote(first, x_ref.at[part, top, :], ext.at[part, far, :], (up, me_c)),
+            remote(first + 1, x_ref.at[part, bottom, :], ext.at[part, pl.ds(0, HALF), :], (down, me_c)),
+        ]
 
     def corners(h):
         part = pl.ds(h * part_groups, part_groups)
-        first = 2 * parts + 2 + 2 * h
+        near = pl.ds(0, HALF)
         return [
-            remote(first, sides.at[:, part, pl.ds(HALF, HALF), :], sides.at[:, part, far, :], (up, me_c)),
-            remote(first + 1, sides.at[:, part, pl.ds(height, HALF), :], sides.at[:, part, pl.ds(0, HALF), :],
-                   (down, me_c)),
+            remote(6 + 4 * h, packed.at[0, part, top, :], sides.at[0, part, far, :], (up, right)),
+            remote(7 + 4 * h, packed.at[1, part, top, :], sides.at[1, part, far, :], (up, left)),
+            remote(8 + 4 * h, packed.at[0, part, bottom, :], sides.at[0, part, near, :], (down, right)),
+            remote(9 + 4 * h, packed.at[1, part, bottom, :], sides.at[1, part, near, :], (down, left)),
         ]
 
     def pack(h):
@@ -133,47 +138,45 @@
             packed[0, h * part_groups + g] = lines[:, :width]
             packed[1, h * part_groups + g] = lines[:, width:]
 
+    pl.semaphore_wait(barrier, len(friends))
+    for i in range(parts):
+        for copy in edges(i):
+            copy.start()
     loads[0].wait()
     loads[1].wait()
-    pack(0)
-    pl.semaphore_wait(barrier, len(friends))
-    for copy in strips(0) + edges:
-        copy.start()
-    for load in loads[2:]:
-        load.start()
-    for h in range(1, parts):
+    for h in range(2):
         pack(h)
-        for copy in strips(h):
+        for copy in strips(h) + corners(h):
             copy.start()
-
     loads[2].wait()
-    for copy in edges:
-        copy.wait()
 
     def down_rows(pair):
         both = dot(band_w[...], pair)
         return both[:height] + both[height:]
 
-    def own_rows(i, carry):
+    def own_rows(i):
         for j in range(0, 2 * fold, 2):
             g, s = 2 * i + j // fold, j % fold
-            start = pl.ds(pl.multiple_of(g * height, 16), height)
+            start = pl.ds(g * height, height)
             n = g * fold + s
             result = down_rows(jnp.concatenate([ext[n], ext[n + 1]], axis=1))
             for t in (0, 1):
                 high, low = split_value(result[:, t * width : (t + 1) * width])
                 own_h[s + t, start, :] = high
                 own_l[s + t, start, :] = low
-        return carry
-
-    lax.fori_loop(0, groups // 2, own_rows, 0)
+
+    for i in range(parts):
+        for copy in edges(i):
+            copy.wait()
+        own_rows(i)
     loads[3].wait()
     lane = lax.broadcasted_iota(jnp.int32, (height, width), 1)
     even = lax.rem(lane // HALF, 2) == 0
 
-    def finish(h):
-        for copy in corners(h):
+    for h in range(2):
+        for copy in strips(h) + corners(h):
             copy.wait()
+
         for g in range(h * part_groups, (h + 1) * part_groups):
             result = down_rows(jnp.concatenate([sides[0, g], sides[1, g]], axis=1))
             before, after = result[:, :width], result[:, width:]
@@ -197,15 +200,6 @@
             return carry
 
         lax.fori_loop(0, fold // 2, columns, 0)
-
-    for h in range(parts):
-        for copy in strips(h):
-            copy.wait()
-        for copy in corners(h):
-            copy.start()
-        if h > 0:
-            finish(h - 1)
-    finish(parts - 1)
 
     step = 16 if height % 16 == 0 else 2
 
@@ -309,8 +303,6 @@
     r_ref[...] = both[:, :count]
     high, low = split_value(both[:, count:])
     twice = jnp.concatenate([high, high], axis=1)
-    once = jnp.concatenate([low, jnp.zeros_like(low)], axis=1)
-    inverse = jnp.concatenate([twice, once], axis=0)
     load.wait()
     stores = []
     for c in range(height // chunk):
@@ -318,8 +310,7 @@
         for i in range(0, chunk, 2):
             row = c * chunk + i
             pair = jnp.concatenate([field[row], field[row + 1]], axis=1)
-            result = dot(inverse, pair)
-            result = result[:count] + result[count:]
+            result = dot(twice, pair) + dot(low, pair[:count])
             for t in range(2):
                 view[pl.ds(i + t, count, stride=chunk), :] = result[:, t * width : (t + 1) * width]
         store = pltpu.make_async_copy(basis.at[c], q_hbm.at[:, pl.ds(c * chunk, chunk), :], store_sem.at[c])
@@ -365,7 +356,7 @@
             pltpu.VMEM((rows,) + piece, F32),
             pltpu.VMEM((cols,) + piece, F32),
             pltpu.VMEM((rows,) + piece, F32),
-            dma((4,)), dma((18,)), dma((18,)), dma((rows,)), dma((rows,)), dma((cols,)), dma((cols,)),
+            dma((4,)), dma((14 + groups,)), dma((14 + groups,)), dma((rows,)), dma((rows,)), dma((cols,)), dma((cols,)),
             dma((rows,)), dma((rows,)), dma,
         ],
         compiler_params=pltpu.CompilerParams(

time: 42.2 us -> 39.9 us (0.945)
  Pallas kernels: 41.3 us -> 39.1 us
    pallas_call x1, Pallas kernels: 36 us -> 33.7 us  [local(): pl.pallas_call(functools.partial(filter_kernel, rows, cols), out_shape=(j...]
where the time goes in v4:
time: 39.9 us; the launch traced here: 39.7 us
  Pallas kernels  39.1 us (98%)
  between operations  0.64 us (2%)
    pallas_call x1, Pallas kernels, local(): pl.pallas_call(functools.partial(filter_kernel, rows, cols), out_shape=(j...  33.7 us
    pallas_call x1, Pallas kernels, local(): pl.pallas_call(functools.partial(basis_kernel, chunk), out_shape=(jax.Sha...  5.33 us

profile of v4, /device:TPU:0, one launch (start us, length us, event | category | flops | bytes accessed | tf_op | source)
XLA Modules:
  0.0 39.7 jit_solution(10082156616484881278)
XLA Ops:
  0.6 33.7 %shard_map.59 = (bf16[96,128,128]{2,1,0:T(8,128)(2,1)}, f32[32,128]{1,0:T(8,128)}) custom-call(bf16[64,96,128]{2,1,0:T(8,128)(2,1)} %x_ref.1, bf16[1024,256]{1,0:T(8,128)(2,1)} %constant.6.clone.pick_hbm, bf16[8,256,256]{2,1,0:T(8,128)(2,1)} %constant.7.clone.joint_hbm, bf16[192,128]{1,0:T(8,128)(2,1)} %constant.8.clone.band_hbm), custom_call_target="tpu_custom_call" | custom-call | tf_op jit(solution)/shard_map/pallas_call | solution.py:337
  34.4 5.3 %shard_map.60 = (f32[64,96,128]{2,1,0:T(8,128)}, f32[64,64]{1,0:T(8,128)}) custom-call(f32[32,128]{1,0:T(8,128)} %get-tuple-element.4.gram_ref, bf16[96,128,128]{2,1,0:T(8,128)(2,1)} %get-tuple-element.5.field_hbm), custom_call_target="tpu_custom_call" | custom-call | tf_op jit(solution)/shard_map/pallas_call | solution.py:366
